TPU v7x, 32 devices: a whole 2x2x4 slice. The times are simulated.
32 devices in a mesh: depth: 2 (over x), row: 4 (over z), col: 4 (over y, core).
Axes of the slice: x: 2, y: 2, z: 4, core: 2. Of those that a mesh axis runs over, the one named last changes fastest.
Arguments:
- context: bfloat16 [1024, 12288], P(('depth', 'row'), 'col'), may hold values from -6 to 6
- d_out: bfloat16 [1024, 12288], P(('depth', 'col'), 'row'), may hold values from -6 to 6
- out_weight: bfloat16 [12288, 12288], P('col', 'row'), may hold values from -0.0546875 to 0.0546875
Outputs:
- d_context: bfloat16 [1024, 12288], P(('depth', 'row'), 'col')
- d_weight: bfloat16 [12288, 12288], P('col', 'row')
All inputs are finite; a program needn't handle non-finite values.
Results may differ from a plain program's by a relative error of at most 0.02.
Values may be sent and summed in bfloat16 or wider, within the bound.
A program may use at most 128 MiB of HBM per device.

v0:
```python
import jax
import jax.numpy as jnp
from jax import lax
from jax.sharding import PartitionSpec as P


def on_device(context, d_out, out_weight):
    grad_rows = lax.all_gather(d_out, "col", axis=0, tiled=True)
    d_context = lax.psum_scatter(
        lax.dot_general(
            grad_rows, out_weight, (((1,), (1,)), ((), ())), preferred_element_type=jnp.float32
        ).astype(jnp.bfloat16),
        "row",
        scatter_dimension=0,
        tiled=True,
    )
    partial_weight = lax.dot_general(
        lax.all_gather(context, "row", axis=0, tiled=True),
        grad_rows,
        (((0,), (0,)), ((), ())),
        preferred_element_type=jnp.float32,
    )
    d_weight = lax.psum(partial_weight.astype(jnp.bfloat16), "depth")
    return (d_context, d_weight)


def solution(mesh):
    in_specs = (P(("depth", "row"), "col"), P(("depth", "col"), "row"), P("col", "row"))
    out_specs = (P(("depth", "row"), "col"), P("col", "row"))
    return jax.shard_map(
        on_device, mesh=mesh, in_specs=in_specs, out_specs=out_specs, check_vma=False
    )
```

profile of v0, /device:TPU:10, one launch (start us, length us, event | category | flops | bytes accessed | tf_op | source)
XLA Modules:
  0.0 615.5 jit_solution(14418755424796113299)
XLA Ops:
  7.2 0.0 all-gather.3.cloned.1.call-start
  7.2 0.7 all-gather.3.cloned.1.call-update
  7.9 0.0 all-gather.5.cloned.1.call-start
  7.9 0.7 all-gather.5.cloned.1.call-update
  8.6 0.0 reduce-scatter.2.cloned.1.call-start
  8.7 30.6 %all-gather.3.cloned.1.call-done = bf16[512,3072]{1,0:T(8,128)(2,1)} async-done(((bf16[128,3072]{1,0:T(8,128)(2,1)}), bf16[512,3072]{1,0:T(8,128)(2,1)}) %all-gather.3.cloned.1.call-update) | async-done | bytes 3145744 | tf_op jit(solution)/shard_map/all_gather | solution.py:8
  39.3 15.9 %convolution_convert_fusion.1 = bf16[512,3072]{1,0:T(8,128)(2,1)} fusion(bf16[512,3072]{1,0:T(8,128)(2,1)} %all-gather.3.cloned.1.call-done, bf16[3072,3072]{1,0:T(8,128)(2,1)} %param.5), kind=kOutput, calls=%fused_computation.1 | convolution fusion | flops 9665249280 | bytes 25165824 | tf_op jit(solution)/shard_map/dot_general | solution.py:10
  55.2 0.0 copy-start
  55.2 0.0 reduce-scatter.2.cloned.1.call-update
  55.2 0.0 all-reduce.2.cloned.1.call-start
  55.3 46.8 %all-gather.5.cloned.1.call-done = bf16[512,3072]{1,0:T(8,128)(2,1)} async-done(((bf16[128,3072]{1,0:T(8,128)(2,1)}), bf16[512,3072]{1,0:T(8,128)(2,1)}) %all-gather.5.cloned.1.call-update) | async-done | bytes 3145744 | tf_op jit(solution)/shard_map/all_gather | solution.py:18
  102.1 0.0 copy-done
  102.1 15.0 %convolution_convert_fusion = bf16[3072,3072]{1,0:T(8,128)(2,1)} fusion(bf16[512,3072]{1,0:T(8,128)(2,1)} %all-gather.5.cloned.1.call-done, bf16[512,3072]{1,0:T(8,128)(2,1)S(1)} %copy-done), kind=kOutput, calls=%fused_computation | convolution fusion | flops 9673113600 | bytes 25165824 | tf_op jit(solution)/shard_map/dot_general | solution.py:17
  117.1 0.0 all-reduce.2.cloned.1.call-update
  117.2 48.5 %reduce-scatter.2.cloned.1.call-done = bf16[128,3072]{1,0:T(8,128)(2,1)} async-done(((bf16[512,3072]{1,0:T(8,128)(2,1)}), bf16[128,3072]{1,0:T(8,128)(2,1)}) %reduce-scatter.2.cloned.1.call-update) | async-done | bytes 786448 | tf_op jit(solution)/shard_map/reduce_scatter | solution.py:9
  165.7 426.7 %all-reduce.2.cloned.1.call-done = bf16[3072,3072]{1,0:T(8,128)(2,1)} async-done(((bf16[3072,3072]{1,0:T(8,128)(2,1)}), bf16[3072,3072]{1,0:T(8,128)(2,1)}) %all-reduce.2.cloned.1.call-update) | async-done | bytes 18874384 | tf_op jit(solution)/shard_map/psum | solution.py:23
  592.4 16.6 %copy.6 = bf16[3072,3072]{1,0:T(8,128)(2,1)} copy(bf16[3072,3072]{1,0:T(8,128)(2,1)} %all-reduce.2.cloned.1.call-done) | data formatting | bytes 37748736
Async XLA Ops:
  7.2 32.1 %all-gather.3.cloned.1.call-start = ((), (), s32[]{:S(2)}) async-start(), calls=%async_computation.1 | async-start | bytes 3932160 | tf_op jit(solution)/shard_map/all_gather | solution.py:8
  7.9 94.2 %all-gather.5.cloned.1.call-start = ((), (), s32[]{:S(2)}) async-start(), calls=%async_computation.3 | async-start | bytes 3932160 | tf_op jit(solution)/shard_map/all_gather | solution.py:18
  8.6 157.1 %reduce-scatter.2.cloned.1.call-start = ((), (), s32[]{:S(2)}) async-start(), calls=%async_computation.2 | async-start | bytes 3932160 | tf_op jit(solution)/shard_map/reduce_scatter | solution.py:9
  55.2 46.9 %copy-start = (bf16[512,3072]{1,0:T(8,128)(2,1)S(1)}, bf16[512,3072]{1,0:T(8,128)(2,1)}, u32[]{:S(2)}) copy-start(bf16[512,3072]{1,0:T(8,128)(2,1)} %all-gather.3.cloned.1.call-done) | copy-start | bytes 9437188
  55.2 537.1 %all-reduce.2.cloned.1.call-start = ((), (), s32[]{:S(2)}) async-start(), calls=%async_computation.4 | async-start | bytes 37748736 | tf_op jit(solution)/shard_map/psum | solution.py:23
Sparse Core Ops, SparseCore 0:
  9.6 29.6 all-gather.2
  40.8 61.2 all-gather.4
  105.0 60.6 reduce-scatter.1
  168.6 423.7 all-reduce.1
where the time goes:
time: 617 us; the launch traced here: 616 us
  waiting for transfers between devices  554 us (90%)
  matrix products  31 us (5%)
  local copies, waits for them, and re-layouts  16.6 us (3%)
  between operations  13.8 us (2%)
    psum x1, waiting for transfers between devices, on_device(): d_weight = lax.psum(partial_weight.astype(jnp.bfloat16), 'depth')  427 us
    reduce_scatter x1, waiting for transfers between devices, on_device(): lax.psum_scatter(lax.dot_general(grad_rows, out_weight, (((1,), (1,)), ((...  48.5 us
    all_gather x1, waiting for transfers between devices, on_device(): lax.all_gather(context, 'row', axis=0, tiled=True)  46.8 us
    all_gather x1, waiting for transfers between devices, on_device(): grad_rows = lax.all_gather(d_out, 'col', axis=0, tiled=True)  30.6 us
    unnamed x3, local copies, waits for them, and re-layouts  16.6 us
    dot_general x1, matrix products, on_device(): lax.dot_general(grad_rows, out_weight, (((1,), (1,)), ((), ())), preferre...  15.9 us
    dot_general x1, matrix products, on_device(): lax.dot_general(lax.all_gather(context, 'row', axis=0, tiled=True), grad_...  15 us
  transfers between devices with their start and end apart: 4, of which 4 were waited for; matrix products, arithmetic and copies ran while one was open for 5% of the time, Pallas kernels for 0%

commit v1 on v0

--- a/solution.py
+++ b/solution.py
@@ -6,6 +6,10 @@
 
 def on_device(context, d_out, out_weight):
     grad_rows = lax.all_gather(d_out, "col", axis=0, tiled=True)
+    other_depth = lax.ppermute(d_out, "depth", [(0, 1), (1, 0)])
+    other_rows = lax.all_gather(other_depth, "col", axis=0, tiled=True)
+    context_rows = lax.all_gather(context, "row", axis=0, tiled=True)
+    other_context = lax.ppermute(context_rows, "depth", [(0, 1), (1, 0)])
     d_context = lax.psum_scatter(
         lax.dot_general(
             grad_rows, out_weight, (((1,), (1,)), ((), ())), preferred_element_type=jnp.float32
@@ -14,13 +18,12 @@
         scatter_dimension=0,
         tiled=True,
     )
-    partial_weight = lax.dot_general(
-        lax.all_gather(context, "row", axis=0, tiled=True),
-        grad_rows,
+    d_weight = lax.dot_general(
+        jnp.concatenate([context_rows, other_context], axis=0),
+        jnp.concatenate([grad_rows, other_rows], axis=0),
         (((0,), (0,)), ((), ())),
         preferred_element_type=jnp.float32,
-    )
-    d_weight = lax.psum(partial_weight.astype(jnp.bfloat16), "depth")
+    ).astype(jnp.bfloat16)
     return (d_context, d_weight)
 
 

time: 617 us -> 205 us (0.33)
  waiting for transfers between devices: 554 us -> 145 us
  local copies, waits for them, and re-layouts: 16.6 us -> 0.88 us
  matrix products: 31 us -> 42.1 us
    psum x1 -> x0, waiting for transfers between devices: 427 us -> none  [on_device(): d_weight = lax.psum(partial_weight.astype(jnp.bfloat16), 'depth')]
    ppermute x0 -> x2, waiting for transfers between devices: none -> 27.3 us  [the longest x1 19 us: on_device(): other_depth = lax.ppermute(d_out, 'depth', [(0, 1), (1, 0)])]
    reduce_scatter x1, waiting for transfers between devices: 48.5 us -> 28.1 us  [on_device(): lax.psum_scatter(lax.dot_general(grad_rows, out_weight, (((1,), (1,)), ((...]
    unnamed x3 -> x4, local copies, waits for them, and re-layouts: 16.6 us -> 0.88 us
    dot_general x1, matrix products: 15 us -> 26.1 us  [on_device(): lax.dot_general(jnp.concatenate([context_rows, other_context], axis=0), j...]
    all_gather x1 -> x2, waiting for transfers between devices: 46.8 us -> 57.5 us  [the longest x1 42.8 us: on_device(): context_rows = lax.all_gather(context, 'row', axis=0, tiled=True)]
  transfers between devices with their start and end apart: 4 -> 6, of which waited for: 4 -> 6; matrix products, arithmetic and copies ran while one was open for 5% -> 21% of each run, Pallas kernels for 0% -> 0%
where the time goes in v1:
time: 205 us; the launch traced here: 203 us
  waiting for transfers between devices  145 us (71%)
  matrix products  42.1 us (21%)
  between operations  13.8 us (7%)
    all_gather x1, waiting for transfers between devices, on_device(): context_rows = lax.all_gather(context, 'row', axis=0, tiled=True)  42.8 us
    all_gather x1, waiting for transfers between devices, on_device(): grad_rows = lax.all_gather(d_out, 'col', axis=0, tiled=True)  30.5 us
    reduce_scatter x1, waiting for transfers between devices, on_device(): lax.psum_scatter(lax.dot_general(grad_rows, out_weight, (((1,), (1,)), ((...  28.1 us
    dot_general x1, matrix products, on_device(): lax.dot_general(jnp.concatenate([context_rows, other_context], axis=0), j...  26.1 us
    ppermute x1, waiting for transfers between devices, on_device(): other_depth = lax.ppermute(d_out, 'depth', [(0, 1), (1, 0)])  19 us
    dot_general x1, matrix products, on_device(): lax.dot_general(grad_rows, out_weight, (((1,), (1,)), ((), ())), preferre...  15.9 us
    all_gather x1, waiting for transfers between devices, on_device(): other_rows = lax.all_gather(other_depth, 'col', axis=0, tiled=True)  14.7 us
    ppermute x1, waiting for transfers between devices, on_device(): other_context = lax.ppermute(context_rows, 'depth', [(0, 1), (1, 0)])  8.3 us
  transfers between devices with their start and end apart: 6, of which 6 were waited for; matrix products, arithmetic and copies ran while one was open for 21% of the time, Pallas kernels for 0%

profile of v1, /device:TPU:10, one launch (start us, length us, event | category | flops | bytes accessed | tf_op | source)
XLA Modules:
  0.0 202.8 jit_solution(7674799886485145745)
XLA Ops:
  7.2 0.0 all-gather.6.cloned.1.call-start
  7.2 0.7 all-gather.6.cloned.1.call-update
  7.9 0.0 all-gather.4.cloned.1.call-start
  7.9 0.7 all-gather.4.cloned.1.call-update
  8.6 0.0 all-gather.8.cloned.1.call-start
  8.7 0.6 collective-permute-start.1
  9.3 19.0 %collective-permute-done.1 = bf16[128,3072]{1,0:T(8,128)(2,1)S(1)} collective-permute-done((bf16[128,3072]{1,0:T(8,128)(2,1)}, bf16[128,3072]{1,0:T(8,128)(2,1)S(1)}, u32[]{:S(2)}, u32[]{:S(2)}) %collective-permute-start.1) | collective-permute-done | bytes 786464 | tf_op jit(solution)/shard_map/ppermute | solution.py:9
  28.2 0.0 copy-start
  28.3 0.9 copy-done
  29.1 0.0 all-gather.8.cloned.1.call-update
  29.2 0.0 reduce-scatter.2.cloned.1.call-start
  29.2 42.8 %all-gather.6.cloned.1.call-done = bf16[512,3072]{1,0:T(8,128)(2,1)} async-done(((bf16[128,3072]{1,0:T(8,128)(2,1)}), bf16[512,3072]{1,0:T(8,128)(2,1)}) %all-gather.6.cloned.1.call-update) | async-done | bytes 3145744 | tf_op jit(solution)/shard_map/all_gather | solution.py:11
  72.0 0.0 copy-start.1
  72.0 0.5 collective-permute-start
  72.5 30.5 %all-gather.4.cloned.1.call-done = bf16[512,3072]{1,0:T(8,128)(2,1)} async-done(((bf16[128,3072]{1,0:T(8,128)(2,1)}), bf16[512,3072]{1,0:T(8,128)(2,1)}) %all-gather.4.cloned.1.call-update) | async-done | bytes 3145744 | tf_op jit(solution)/shard_map/all_gather | solution.py:8
  103.0 15.9 %convolution_convert_fusion.1 = bf16[512,3072]{1,0:T(8,128)(2,1)} fusion(bf16[512,3072]{1,0:T(8,128)(2,1)} %all-gather.4.cloned.1.call-done, bf16[3072,3072]{1,0:T(8,128)(2,1)} %param.5), kind=kOutput, calls=%fused_computation.7 | convolution fusion | flops 9665249280 | bytes 25165824 | tf_op jit(solution)/shard_map/dot_general | solution.py:14
  119.0 0.0 reduce-scatter.2.cloned.1.call-update
  119.0 14.7 %all-gather.8.cloned.1.call-done = bf16[512,3072]{1,0:T(8,128)(2,1)} async-done(((bf16[128,3072]{1,0:T(8,128)(2,1)}), bf16[512,3072]{1,0:T(8,128)(2,1)}) %all-gather.8.cloned.1.call-update) | async-done | bytes 3145744 | tf_op jit(solution)/shard_map/all_gather | solution.py:10
  133.7 8.3 %collective-permute-done = bf16[512,3072]{1,0:T(8,128)(2,1)} collective-permute-done((bf16[512,3072]{1,0:T(8,128)(2,1)}, bf16[512,3072]{1,0:T(8,128)(2,1)}, u32[]{:S(2)}, u32[]{:S(2)}) %collective-permute-start) | collective-permute-done | bytes 3145760 | tf_op jit(solution)/shard_map/ppermute | solution.py:12
  142.0 0.0 copy-done.1
  142.0 26.1 %convolution_convert_fusion = bf16[3072,3072]{1,0:T(8,128)(2,1)} fusion(bf16[512,3072]{1,0:T(8,128)(2,1)} %collective-permute-done, bf16[512,3072]{1,0:T(8,128)(2,1)S(1)} %copy-done.1, bf16[512,3072]{1,0:T(8,128)(2,1)} %all-gather.8.cloned.1.call-done, bf16[512,3072]{1,0:T(8,128)(2,1)} %all-gather.4.cloned.1.call-done), kind=kOutput, calls=%fused_computation | convolution fusion | flops 19361955840 | bytes 31457280 | tf_op jit(solution)/shard_map/dot_general | solution.py:21
  168.2 28.1 %reduce-scatter.2.cloned.1.call-done = bf16[128,3072]{1,0:T(8,128)(2,1)} async-done(((bf16[512,3072]{1,0:T(8,128)(2,1)}), bf16[128,3072]{1,0:T(8,128)(2,1)}) %reduce-scatter.2.cloned.1.call-update) | async-done | bytes 786448 | tf_op jit(solution)/shard_map/reduce_scatter | solution.py:13
Async XLA Ops:
  7.2 64.8 %all-gather.6.cloned.1.call-start = ((), (), s32[]{:S(2)}) async-start(), calls=%async_computation.3 | async-start | bytes 3932160 | tf_op jit(solution)/shard_map/all_gather | solution.py:11
  7.9 95.1 %all-gather.4.cloned.1.call-start = ((), (), s32[]{:S(2)}) async-start(), calls=%async_computation.1 | async-start | bytes 3932160 | tf_op jit(solution)/shard_map/all_gather | solution.py:8
  8.6 125.1 %all-gather.8.cloned.1.call-start = ((), (), s32[]{:S(2)}) async-start(), calls=%async_computation.4 | async-start | bytes 3932160 | tf_op jit(solution)/shard_map/all_gather | solution.py:10
  8.7 19.6 %collective-permute-start.1 = (bf16[128,3072]{1,0:T(8,128)(2,1)}, bf16[128,3072]{1,0:T(8,128)(2,1)S(1)}, u32[]{:S(2)}, u32[]{:S(2)}) collective-permute-start(bf16[128,3072]{1,0:T(8,128)(2,1)} %param.4), channel_id=1, source_target_pairs={{0,16},{16,0},{1,17},{17,1},{2,18},{18,2},{3,19},{19,3},{4,20},{20... | collective-permute-start | bytes 2359304 | tf_op jit(solution)/shard_map/ppermute | solution.py:9
  28.2 0.9 copy-start
  29.2 167.1 %reduce-scatter.2.cloned.1.call-start = ((), (), s32[]{:S(2)}) async-start(), calls=%async_computation.2 | async-start | bytes 3932160 | tf_op jit(solution)/shard_map/reduce_scatter | solution.py:13
  72.0 70.1 %copy-start.1 = (bf16[512,3072]{1,0:T(8,128)(2,1)S(1)}, bf16[512,3072]{1,0:T(8,128)(2,1)}, u32[]{:S(2)}) copy-start(bf16[512,3072]{1,0:T(8,128)(2,1)} %all-gather.6.cloned.1.call-done) | copy-start | bytes 9437188
  72.0 70.1 %collective-permute-start = (bf16[512,3072]{1,0:T(8,128)(2,1)}, bf16[512,3072]{1,0:T(8,128)(2,1)}, u32[]{:S(2)}, u32[]{:S(2)}) collective-permute-start(bf16[512,3072]{1,0:T(8,128)(2,1)} %all-gather.6.cloned.1.call-done), channel_id=1, source_target_pairs={{0,16},{16,0},{1,17},{17,1},{2,18},{18,2},{3,19},{19,3},{4,20},{20... | collective-permute-start | bytes 9437192 | tf_op jit(solution)/shard_map/ppermute | solution.py:12
Sparse Core Ops, SparseCore 0:
  9.6 62.3 all-gather.5
  73.5 29.4 all-gather.3
  105.2 28.5 all-gather.7
  136.5 59.7 reduce-scatter.1

commit v2 on v1

v2 whole, which is shorter than its diff:
```python
import functools

import jax
import jax.numpy as jnp
from jax import lax
from jax.experimental import pallas as pl
from jax.experimental.pallas import tpu as pltpu
from jax.sharding import PartitionSpec as P

MESH = pl.DeviceIdType.MESH
PIECES = 2


def kernel(
    R, C, ctx_in, dout_in, w_in, ctx_all, dout_all, dctx,
    wv, dv, part, sbuf, rbuf,
    w_sem, own_sem, load_sem,
    c_recv, c_right, c_left, c_x,
    g_recv, g_right, g_left, g_core, g_x,
    r_recv, r_send,
):
    T = ctx_in.shape[0]
    tp = T // PIECES
    Y = C // 2
    x, z, c = lax.axis_index("depth"), lax.axis_index("row"), lax.axis_index("col")
    y = c // 2
    core = c - 2 * y
    mate = c + 1 - 2 * core
    halves = range(PIECES)

    to_x, to_core = {"depth": 1 - x}, {"col": mate}
    to_right, to_left = {"row": z + 1}, {"row": z - 1}
    to_yr, to_yl = {"col": c + 2}, {"col": c - 2}

    barrier = pltpu.get_barrier_semaphore()

    def greet(device):
        pl.semaphore_signal(barrier, inc=1, device_id=device, device_id_type=MESH)

    greet(to_x)
    greet(to_core)
    pl.when(z < R - 1)(lambda: greet(to_right))
    pl.when(z > 0)(lambda: greet(to_left))
    pl.when(y < Y - 1)(lambda: greet(to_yr))
    pl.when(y > 0)(lambda: greet(to_yl))
    count = 2
    for there in (z < R - 1, z > 0, y < Y - 1, y > 0):
        count = count + there.astype(jnp.int32)

    wr = w_in.shape[0] // 4
    w_copies = [
        pltpu.make_async_copy(w_in.at[pl.ds(i * wr, wr)], wv.at[pl.ds(i * wr, wr)], w_sem.at[i])
        for i in range(4)
    ]
    own_copies = [
        pltpu.make_async_copy(dout_in, dv.at[pl.ds(c * T, T)], own_sem.at[0]),
        pltpu.make_async_copy(dout_in, dout_all.at[pl.ds((x * C + c) * T, T)], own_sem.at[1]),
        pltpu.make_async_copy(ctx_in, ctx_all.at[pl.ds((x * R + z) * T, T)], own_sem.at[2]),
    ]
    for copy in [own_copies[0]] + w_copies + own_copies[1:]:
        copy.start()

    def rows(block, p):
        return pl.ds(block * T + p * tp, tp)

    def depth_of(k):
        return x if k == 0 else 1 - x

    def remote(src, dst, send, recv, device):
        return pltpu.make_async_remote_copy(
            src_ref=src, dst_ref=dst, send_sem=send, recv_sem=recv, device_id=device, device_id_type=MESH
        )

    def c_copy(way, r, p, own=False):
        dst = ctx_all.at[rows(x * R + r, p)]
        src = ctx_in.at[rows(0, p)] if own else dst
        if way == "x":
            return remote(src, dst, c_x.at[r, p], c_recv.at[1, r, p], to_x)
        if way == "right":
            return remote(src, dst, c_right.at[r, p], c_recv.at[0, r, p], to_right)
        return remote(src, dst, c_left.at[r, p], c_recv.at[0, r, p], to_left)

    def c_wait(k, r, p):
        there = ctx_all.at[rows(depth_of(k) * R + r, p)]
        remote(there, there, c_x.at[r, p], c_recv.at[k, r, p], to_x).wait_recv()

    def g_copy(way, k, b, p, own=False):
        dst = dout_all.at[rows(depth_of(k) * C + b, p)]
        src = dout_in.at[rows(0, p)] if own else dst
        if way == "x":
            return remote(src, dst, g_x.at[p], g_recv.at[1, b, p], to_x)
        send, device = {"right": (g_right, to_yr), "left": (g_left, to_yl), "core": (g_core, to_core)}[way]
        return remote(src, dst, send.at[k, b, p], g_recv.at[k, b, p], device)

    def g_wait(k, b, p):
        there = dout_all.at[rows(depth_of(k) * C + b, p)]
        remote(there, there, g_core.at[k, b, p], g_recv.at[k, b, p], to_core).wait_recv()

    def g_sends(k, b, p, own=False):
        pl.when(y < Y - 1)(lambda: g_copy("right", k, b, p, own).start())
        pl.when(y > 0)(lambda: g_copy("left", k, b, p, own).start())
        g_copy("core", k, b, p, own).start()

    pl.semaphore_wait(barrier, count)

    for p in halves:
        g_sends(0, c, p, own=True)
        g_copy("x", 0, c, p, own=True).start()
    for p in halves:
        pl.when(z < R - 1)(lambda: c_copy("right", z, p, own=True).start())
        pl.when(z > 0)(lambda: c_copy("left", z, p, own=True).start())
        c_copy("x", z, p, own=True).start()

    def c_step(s):
        def arrived(r, way, more):
            for p in halves:
                c_wait(0, r, p)
                pl.when(more)(lambda: c_copy(way, r, p).start())
                c_copy("x", r, p).start()

        pl.when(z - 1 - s >= 0)(lambda: arrived(z - 1 - s, "right", z < R - 1))
        pl.when(z + 1 + s <= R - 1)(lambda: arrived(z + 1 + s, "left", z > 0))

    def g_step(k, s):
        def arrived(b, way, more):
            for p in halves:
                g_wait(k, b, p)
                pl.when(more)(lambda: g_copy(way, k, b, p).start())
                g_copy("core", k, b, p).start()

        pl.when(y - 1 - s >= 0)(lambda: arrived(c - 2 - 2 * s, "right", y < Y - 1))
        pl.when(y + 1 + s <= Y - 1)(lambda: arrived(c + 2 + 2 * s, "left", y > 0))

    def load(block, count_of, which):
        return pltpu.make_async_copy(
            dout_all.at[pl.ds((x * C + block) * T, count_of * T)],
            dv.at[pl.ds(block * T, count_of * T)],
            load_sem.at[which],
        )

    tn = 512 if wv.shape[0] % 512 == 0 else 256

    def multiply(pair):
        tokens = pl.ds(pair * 2 * T, 2 * T)

        @pl.loop(0, wv.shape[0] // tn)
        def _(i):
            columns = pl.ds(pl.multiple_of(i * tn, tn), tn)
            part[tokens, columns] = lax.dot_general(
                dv[tokens, :], wv[columns, :], (((1,), (1,)), ((), ())), preferred_element_type=jnp.float32
            )

    for p in halves:
        g_wait(0, mate, p)
    load(mate, 1, 0).start()
    own_copies[0].wait()
    for copy in w_copies:
        copy.wait()
    load(mate, 1, 0).wait()
    multiply(y)

    c_step(0)
    for p in halves:
        g_wait(1, c, p)
        g_sends(1, c, p)

    def far_pair(s):
        def take(pair, which):
            for p in halves:
                g_wait(0, 2 * pair + 1 - core, p)
            load(2 * pair, 2, which).start()
            load(2 * pair, 2, which).wait()
            multiply(pair)

        pl.when(y - 1 - s >= 0)(lambda: take(y - 1 - s, 1))
        pl.when(y + 1 + s <= Y - 1)(lambda: take(y + 1 + s, 2))

    for s in range(Y - 1):
        g_step(0, s)
        far_pair(s)

    def r_copy(d, p, rightward):
        if rightward:
            return remote(sbuf.at[rows(d, p)], rbuf.at[rows(d, p)], r_send.at[d, p], r_recv.at[d, p], to_right)
        slot = jnp.where(z - 1 == d, R, d)
        return remote(sbuf.at[rows(d, p)], rbuf.at[rows(slot, p)], r_send.at[d, p], r_recv.at[slot, p], to_left)

    def r_wait(slot, p):
        there = rbuf.at[rows(slot, p)]
        remote(there, there, r_send.at[0, p], r_recv.at[slot, p], to_x).wait_recv()

    def r_hop(d, p, rightward, first):
        if first:
            sbuf[rows(d, p), :] = part[rows(d, p), :].astype(jnp.bfloat16)
        else:
            r_wait(d, p)
            total = part[rows(d, p), :] + rbuf[rows(d, p), :].astype(jnp.float32)
            sbuf[rows(d, p), :] = total.astype(jnp.bfloat16)
        r_copy(d, p, rightward).start()

    @pl.when(z == 0)
    def _():
        for d in range(R - 1, 0, -1):
            for p in halves:
                r_hop(d, p, True, True)

    @pl.when(z == R - 1)
    def _():
        for d in range(R - 1):
            for p in halves:
                r_hop(d, p, False, True)

    for s in range(1, R - 1):
        c_step(s)
    for s in range(Y - 1):
        g_step(1, s)

    for i in range(R - 1):
        for p in halves:
            pl.when((z > 0) & (z < R - 1 - i))(lambda: r_hop(R - 1 - i, p, True, False))
            pl.when((z < R - 1) & (z > i))(lambda: r_hop(i, p, False, False))

    def own_rows(slot, p):
        return pl.ds(pl.multiple_of(slot * T + p * tp, tp), tp)

    for p in halves:
        out = pl.ds(p * tp, tp)

        @pl.when(z == 0)
        def _():
            r_wait(R, p)
            dctx[out, :] = (part[own_rows(z, p), :] + rbuf[own_rows(R, p), :].astype(jnp.float32)).astype(jnp.bfloat16)

        @pl.when(z == R - 1)
        def _():
            r_wait(z, p)
            dctx[out, :] = (part[own_rows(z, p), :] + rbuf[own_rows(z, p), :].astype(jnp.float32)).astype(jnp.bfloat16)

        @pl.when((z > 0) & (z < R - 1))
        def _():
            r_wait(z, p)
            r_wait(R, p)
            both = rbuf[own_rows(z, p), :].astype(jnp.float32) + rbuf[own_rows(R, p), :].astype(jnp.float32)
            dctx[out, :] = (part[own_rows(z, p), :] + both).astype(jnp.bfloat16)

    for p in halves:
        for b in range(Y):
            g_wait(1, 2 * b + 1 - core, p)
        for r in range(R):
            c_wait(1, r, p)
    own_copies[1].wait()
    own_copies[2].wait()
    for p in halves:
        g_copy("x", 0, c, p).wait_send()
        for k in range(2):
            for b in range(Y):
                block = 2 * b + core
                g_copy("core", k, block, p).wait_send()
                pl.when((y < Y - 1) & (b <= y))(lambda: g_copy("right", k, block, p).wait_send())
                pl.when((y > 0) & (b >= y))(lambda: g_copy("left", k, block, p).wait_send())
        for r in range(R):
            c_copy("x", r, p).wait_send()
            pl.when((z < R - 1) & (r <= z))(lambda: c_copy("right", r, p).wait_send())
            pl.when((z > 0) & (r >= z))(lambda: c_copy("left", r, p).wait_send())
            pl.when(z != r)(lambda: r_copy(r, p, True).wait_send())


def exchange(R, C, context, d_out, out_weight):
    T, FC = context.shape
    FR = d_out.shape[1]
    bf16, dma = jnp.bfloat16, pltpu.SemaphoreType.DMA
    hbm, vmem = pl.BlockSpec(memory_space=pl.ANY), pl.BlockSpec(memory_space=pltpu.VMEM)
    return pl.pallas_call(
        functools.partial(kernel, R, C),
        out_shape=(
            jax.ShapeDtypeStruct((2 * R * T, FC), bf16),
            jax.ShapeDtypeStruct((2 * C * T, FR), bf16),
            jax.ShapeDtypeStruct((T, FC), bf16),
        ),
        in_specs=[hbm, hbm, hbm],
        out_specs=(hbm, hbm, vmem),
        scratch_shapes=[
            pltpu.VMEM((FC, FR), bf16),
            pltpu.VMEM((C * T, FR), bf16),
            pltpu.VMEM((C * T, FC), jnp.float32),
            pltpu.VMEM((R * T, FC), bf16),
            pltpu.VMEM(((R + 1) * T, FC), bf16),
            dma((4,)), dma((3,)), dma((3,)),
            dma((2, R, PIECES)), dma((R, PIECES)), dma((R, PIECES)), dma((R, PIECES)),
            dma((2, C, PIECES)), dma((2, C, PIECES)), dma((2, C, PIECES)), dma((2, C, PIECES)), dma((PIECES,)),
            dma((R + 1, PIECES)), dma((R, PIECES)),
        ],
        compiler_params=pltpu.CompilerParams(
            collective_id=0, has_side_effects=True, vmem_limit_bytes=56 * 1024 * 1024
        ),
        cost_estimate=pl.CostEstimate(
            flops=2 * C * T * FC * FR, bytes_accessed=2 * FC * FR, transcendentals=0
        ),
    )(context, d_out, out_weight)


def on_device(R, C, context, d_out, out_weight):
    context_rows, grad_rows, d_context = exchange(R, C, context, d_out, out_weight)
    d_weight = lax.dot_general(
        context_rows, grad_rows, (((0,), (0,)), ((), ())), preferred_element_type=jnp.float32
    ).astype(jnp.bfloat16)
    return (d_context, d_weight)


def solution(mesh):
    in_specs = (P(("depth", "row"), "col"), P(("depth", "col"), "row"), P("col", "row"))
    out_specs = (P(("depth", "row"), "col"), P("col", "row"))
    return jax.shard_map(
        functools.partial(on_device, mesh.shape["row"], mesh.shape["col"]),
        mesh=mesh, in_specs=in_specs, out_specs=out_specs, check_vma=False,
    )
```

time: 205 us -> 131 us (0.64)
  waiting for transfers between devices: 145 us -> 0 us
  Pallas kernels: 0 us -> 102 us
  matrix products: 42.1 us -> 26.6 us
  between operations: 13.8 us -> 0.65 us
    pallas_call x0 -> x1, Pallas kernels: none -> 102 us  [exchange(): pl.pallas_call(functools.partial(kernel, R, C), out_shape=(jax.ShapeDtype...]
    all_gather x3 -> x0, waiting for transfers between devices: 88 us -> none  [the longest x1 42.8 us: on_device(): context_rows = lax.all_gather(context, 'row', axis=0, tiled=True)]
    reduce_scatter x1 -> x0, waiting for transfers between devices: 28.1 us -> none  [on_device(): lax.psum_scatter(lax.dot_general(grad_rows, out_weight, (((1,), (1,)), ((...]
    ppermute x2 -> x0, waiting for transfers between devices: 27.3 us -> none  [the longest x1 19 us: on_device(): other_depth = lax.ppermute(d_out, 'depth', [(0, 1), (1, 0)])]
    dot_general x2 -> x1, matrix products: 42.1 us -> 26.6 us  [on_device(): lax.dot_general(context_rows, grad_rows, (((0,), (0,)), ((), ())), prefer...]
  transfers between devices with their start and end apart: 6 -> 0, of which waited for: 6 -> 0; matrix products, arithmetic and copies ran while one was open for 21% -> 0% of each run, Pallas kernels for 0% -> 0%
where the time goes in v2:
time: 131 us; the launch traced here: 130 us
  Pallas kernels  102 us (78%)
  matrix products  26.6 us (20%)
    pallas_call x1, Pallas kernels, exchange(): pl.pallas_call(functools.partial(kernel, R, C), out_shape=(jax.ShapeDtype...  102 us
    dot_general x1, matrix products, on_device(): lax.dot_general(context_rows, grad_rows, (((0,), (0,)), ((), ())), prefer...  26.6 us

profile of v2, /device:TPU:10, one launch (start us, length us, event | category | flops | bytes accessed | tf_op | source)
XLA Modules:
  0.0 129.7 jit_solution(10853991067046650261)
XLA Ops:
  0.6 101.6 %shard_map.50 = (bf16[1024,3072]{1,0:T(8,128)(2,1)}, bf16[1024,3072]{1,0:T(8,128)(2,1)}, bf16[128,3072]{1,0:T(8,128)(2,1)}) custom-call(bf16[128,3072]{1,0:T(8,128)(2,1)} %ctx_in.1, bf16[128,3072]{1,0:T(8,128)(2,1)} %dout_in.1, bf16[3072,3072]{1,0:T(8,128)(2,1)} %w_in.1), custom_call_target="tpu_custom_call" | custom-call | flops 9663676416 | bytes 18874368 | tf_op jit(solution)/shard_map/pallas_call | solution.py:273
  102.2 0.0 copy-start
  102.2 26.6 %convolution_convert_fusion = bf16[3072,3072]{1,0:T(8,128)(2,1)} fusion(bf16[1024,3072]{1,0:T(8,128)(2,1)} %get-tuple-element.6, bf16[1024,3072]{1,0:T(8,128)(2,1)} %get-tuple-element.7), kind=kOutput, calls=%fused_computation | convolution fusion | flops 19336790016 | bytes 31457280 | tf_op jit(solution)/shard_map/dot_general | solution.py:304
  128.8 0.0 copy-done
  128.8 0.9 copy.6
Async XLA Ops:
  102.2 26.6 %copy-start = (bf16[128,3072]{1,0:T(8,128)(2,1)S(1)}, bf16[128,3072]{1,0:T(8,128)(2,1)}, u32[]{:S(2)}) copy-start(bf16[128,3072]{1,0:T(8,128)(2,1)} %get-tuple-element.10) | copy-start | bytes 2359300

commit v3 on v2

--- a/solution.py
+++ b/solution.py
@@ -12,9 +12,9 @@
 
 
 def kernel(
-    R, C, ctx_in, dout_in, w_in, ctx_all, dout_all, dctx,
-    wv, dv, part, sbuf, rbuf,
-    w_sem, own_sem, load_sem,
+    R, C, ctx_in, dout_in, w_in, ctx_other, dout_other, dctx, half_weight,
+    wv, cv, dv, part, sbuf, rbuf, turned, stage,
+    w_sem, own_sem, stage_sem,
     c_recv, c_right, c_left, c_x,
     g_recv, g_right, g_left, g_core, g_x,
     r_recv, r_send,
@@ -27,6 +27,8 @@
     core = c - 2 * y
     mate = c + 1 - 2 * core
     halves = range(PIECES)
+    cuts = [(0, T // 8), (T // 8, T // 2 - T // 8), (T // 2, T // 2)]
+    late = range(1, 3)
 
     to_x, to_core = {"depth": 1 - x}, {"col": mate}
     to_right, to_left = {"row": z + 1}, {"row": z - 1}
@@ -54,46 +56,44 @@
     ]
     own_copies = [
         pltpu.make_async_copy(dout_in, dv.at[pl.ds(c * T, T)], own_sem.at[0]),
-        pltpu.make_async_copy(dout_in, dout_all.at[pl.ds((x * C + c) * T, T)], own_sem.at[1]),
-        pltpu.make_async_copy(ctx_in, ctx_all.at[pl.ds((x * R + z) * T, T)], own_sem.at[2]),
+        pltpu.make_async_copy(ctx_in, cv.at[pl.ds(z * T, T)], own_sem.at[1]),
     ]
     for copy in [own_copies[0]] + w_copies + own_copies[1:]:
         copy.start()
 
     def rows(block, p):
         return pl.ds(block * T + p * tp, tp)
-
-    def depth_of(k):
-        return x if k == 0 else 1 - x
 
     def remote(src, dst, send, recv, device):
         return pltpu.make_async_remote_copy(
             src_ref=src, dst_ref=dst, send_sem=send, recv_sem=recv, device_id=device, device_id_type=MESH
         )
 
-    def c_copy(way, r, p, own=False):
-        dst = ctx_all.at[rows(x * R + r, p)]
-        src = ctx_in.at[rows(0, p)] if own else dst
+    def c_rows(r, p):
+        return pl.ds(r * T + cuts[p][0], cuts[p][1])
+
+    def c_copy(way, k, r, p, own=False):
+        there = (cv, ctx_other)[k].at[c_rows(r, p)]
+        src = ctx_in.at[c_rows(0, p)] if own else there
         if way == "x":
-            return remote(src, dst, c_x.at[r, p], c_recv.at[1, r, p], to_x)
-        if way == "right":
-            return remote(src, dst, c_right.at[r, p], c_recv.at[0, r, p], to_right)
-        return remote(src, dst, c_left.at[r, p], c_recv.at[0, r, p], to_left)
+            return remote(src, ctx_other.at[c_rows(r, p)], c_x.at[r, p], c_recv.at[1, r, p], to_x)
+        send, device = (c_right, to_right) if way == "right" else (c_left, to_left)
+        return remote(src, there, send.at[k, r, p], c_recv.at[k, r, p], device)
 
     def c_wait(k, r, p):
-        there = ctx_all.at[rows(depth_of(k) * R + r, p)]
+        there = (cv, ctx_other)[k].at[c_rows(r, p)]
         remote(there, there, c_x.at[r, p], c_recv.at[k, r, p], to_x).wait_recv()
 
     def g_copy(way, k, b, p, own=False):
-        dst = dout_all.at[rows(depth_of(k) * C + b, p)]
-        src = dout_in.at[rows(0, p)] if own else dst
+        there = (dv, dout_other)[k].at[rows(b, p)]
+        src = dout_in.at[rows(0, p)] if own else there
         if way == "x":
-            return remote(src, dst, g_x.at[p], g_recv.at[1, b, p], to_x)
+            return remote(src, dout_other.at[rows(b, p)], g_x.at[p], g_recv.at[1, b, p], to_x)
         send, device = {"right": (g_right, to_yr), "left": (g_left, to_yl), "core": (g_core, to_core)}[way]
-        return remote(src, dst, send.at[k, b, p], g_recv.at[k, b, p], device)
+        return remote(src, there, send.at[k, b, p], g_recv.at[k, b, p], device)
 
     def g_wait(k, b, p):
-        there = dout_all.at[rows(depth_of(k) * C + b, p)]
+        there = (dv, dout_other)[k].at[rows(b, p)]
         remote(there, there, g_core.at[k, b, p], g_recv.at[k, b, p], to_core).wait_recv()
 
     def g_sends(k, b, p, own=False):
@@ -106,17 +106,22 @@
     for p in halves:
         g_sends(0, c, p, own=True)
         g_copy("x", 0, c, p, own=True).start()
-    for p in halves:
-        pl.when(z < R - 1)(lambda: c_copy("right", z, p, own=True).start())
-        pl.when(z > 0)(lambda: c_copy("left", z, p, own=True).start())
-        c_copy("x", z, p, own=True).start()
+
+    def c_sends(k, p, own):
+        pl.when(z < R - 1)(lambda: c_copy("right", k, z, p, own).start())
+        pl.when(z > 0)(lambda: c_copy("left", k, z, p, own).start())
+
+    for p in range(3):
+        c_copy("x", 0, z, p, own=True).start()
+        c_sends(0, p, own=True)
 
     def c_step(s):
         def arrived(r, way, more):
-            for p in halves:
-                c_wait(0, r, p)
-                pl.when(more)(lambda: c_copy(way, r, p).start())
-                c_copy("x", r, p).start()
+            for k, p in ((0, 0), (0, 1), (0, 2), (1, 0)):
+                c_wait(k, r, p)
+                pl.when(more)(lambda: c_copy(way, k, r, p).start())
+                if p > 0:
+                    c_copy("x", 0, r, p).start()
 
         pl.when(z - 1 - s >= 0)(lambda: arrived(z - 1 - s, "right", z < R - 1))
         pl.when(z + 1 + s <= R - 1)(lambda: arrived(z + 1 + s, "left", z > 0))
@@ -131,13 +136,6 @@
         pl.when(y - 1 - s >= 0)(lambda: arrived(c - 2 - 2 * s, "right", y < Y - 1))
         pl.when(y + 1 + s <= Y - 1)(lambda: arrived(c + 2 + 2 * s, "left", y > 0))
 
-    def load(block, count_of, which):
-        return pltpu.make_async_copy(
-            dout_all.at[pl.ds((x * C + block) * T, count_of * T)],
-            dv.at[pl.ds(block * T, count_of * T)],
-            load_sem.at[which],
-        )
-
     tn = 512 if wv.shape[0] % 512 == 0 else 256
 
     def multiply(pair):
@@ -152,28 +150,26 @@
 
     for p in halves:
         g_wait(0, mate, p)
-    load(mate, 1, 0).start()
     own_copies[0].wait()
     for copy in w_copies:
         copy.wait()
-    load(mate, 1, 0).wait()
     multiply(y)
 
-    c_step(0)
     for p in halves:
         g_wait(1, c, p)
         g_sends(1, c, p)
+    c_wait(1, z, 0)
+    c_sends(1, 0, own=False)
+    c_step(0)
 
     def far_pair(s):
-        def take(pair, which):
+        def take(pair):
             for p in halves:
                 g_wait(0, 2 * pair + 1 - core, p)
-            load(2 * pair, 2, which).start()
-            load(2 * pair, 2, which).wait()
             multiply(pair)
 
-        pl.when(y - 1 - s >= 0)(lambda: take(y - 1 - s, 1))
-        pl.when(y + 1 + s <= Y - 1)(lambda: take(y + 1 + s, 2))
+        pl.when(y - 1 - s >= 0)(lambda: take(y - 1 - s))
+        pl.when(y + 1 + s <= Y - 1)(lambda: take(y + 1 + s))
 
     for s in range(Y - 1):
         g_step(0, s)
@@ -215,7 +211,31 @@
     for s in range(Y - 1):
         g_step(1, s)
 
+    own_copies[1].wait()
+    stripes = cv.shape[1] // tn
+
+    def stage_copy(i):
+        return pltpu.make_async_copy(
+            stage.at[i % 2], half_weight.at[pl.ds(i * tn, tn)], stage_sem.at[i % 2]
+        )
+
+    def stripe(i):
+        if i >= 2:
+            stage_copy(i - 2).wait()
+        turned[...] = cv[:, pl.ds(i * tn, tn)].T
+
+        @pl.loop(0, dv.shape[1] // tn)
+        def _(j):
+            columns = pl.ds(pl.multiple_of(j * tn, tn), tn)
+            stage[i % 2, :, columns] = jnp.dot(
+                turned[...], dv[:, columns], preferred_element_type=jnp.float32
+            ).astype(jnp.bfloat16)
+
+        stage_copy(i).start()
+
     for i in range(R - 1):
+        if i < stripes // 2:
+            stripe(i)
         for p in halves:
             pl.when((z > 0) & (z < R - 1 - i))(lambda: r_hop(R - 1 - i, p, True, False))
             pl.when((z < R - 1) & (z > i))(lambda: r_hop(i, p, False, False))
@@ -243,13 +263,17 @@
             both = rbuf[own_rows(z, p), :].astype(jnp.float32) + rbuf[own_rows(R, p), :].astype(jnp.float32)
             dctx[out, :] = (part[own_rows(z, p), :] + both).astype(jnp.bfloat16)
 
+    for i in range(min(R - 1, stripes // 2), stripes):
+        stripe(i)
+    for i in range(max(stripes - 2, 0), stripes):
+        stage_copy(i).wait()
+
     for p in halves:
         for b in range(Y):
             g_wait(1, 2 * b + 1 - core, p)
+    for p in late:
         for r in range(R):
             c_wait(1, r, p)
-    own_copies[1].wait()
-    own_copies[2].wait()
     for p in halves:
         g_copy("x", 0, c, p).wait_send()
         for k in range(2):
@@ -259,34 +283,44 @@
                 pl.when((y < Y - 1) & (b <= y))(lambda: g_copy("right", k, block, p).wait_send())
                 pl.when((y > 0) & (b >= y))(lambda: g_copy("left", k, block, p).wait_send())
         for r in range(R):
-            c_copy("x", r, p).wait_send()
-            pl.when((z < R - 1) & (r <= z))(lambda: c_copy("right", r, p).wait_send())
-            pl.when((z > 0) & (r >= z))(lambda: c_copy("left", r, p).wait_send())
             pl.when(z != r)(lambda: r_copy(r, p, True).wait_send())
+    c_copy("x", 0, z, 0).wait_send()
+    for p in late:
+        for r in range(R):
+            c_copy("x", 0, r, p).wait_send()
+    for k, p in ((0, 0), (0, 1), (0, 2), (1, 0)):
+        for r in range(R):
+            pl.when((z < R - 1) & (r <= z))(lambda: c_copy("right", k, r, p).wait_send())
+            pl.when((z > 0) & (r >= z))(lambda: c_copy("left", k, r, p).wait_send())
 
 
 def exchange(R, C, context, d_out, out_weight):
     T, FC = context.shape
     FR = d_out.shape[1]
+    tn = 512 if FC % 512 == 0 else 256
     bf16, dma = jnp.bfloat16, pltpu.SemaphoreType.DMA
     hbm, vmem = pl.BlockSpec(memory_space=pl.ANY), pl.BlockSpec(memory_space=pltpu.VMEM)
     return pl.pallas_call(
         functools.partial(kernel, R, C),
         out_shape=(
-            jax.ShapeDtypeStruct((2 * R * T, FC), bf16),
-            jax.ShapeDtypeStruct((2 * C * T, FR), bf16),
+            jax.ShapeDtypeStruct((R * T, FC), bf16),
+            jax.ShapeDtypeStruct((C * T, FR), bf16),
             jax.ShapeDtypeStruct((T, FC), bf16),
+            jax.ShapeDtypeStruct((FC, FR), bf16),
         ),
         in_specs=[hbm, hbm, hbm],
-        out_specs=(hbm, hbm, vmem),
+        out_specs=(hbm, hbm, vmem, hbm),
         scratch_shapes=[
             pltpu.VMEM((FC, FR), bf16),
+            pltpu.VMEM((R * T, FC), bf16),
             pltpu.VMEM((C * T, FR), bf16),
             pltpu.VMEM((C * T, FC), jnp.float32),
             pltpu.VMEM((R * T, FC), bf16),
             pltpu.VMEM(((R + 1) * T, FC), bf16),
-            dma((4,)), dma((3,)), dma((3,)),
-            dma((2, R, PIECES)), dma((R, PIECES)), dma((R, PIECES)), dma((R, PIECES)),
+            pltpu.VMEM((tn, R * T), bf16),
+            pltpu.VMEM((2, tn, FR), bf16),
+            dma((4,)), dma((2,)), dma((2,)),
+            dma((2, R, 3)), dma((2, R, 3)), dma((2, R, 3)), dma((R, 3)),
             dma((2, C, PIECES)), dma((2, C, PIECES)), dma((2, C, PIECES)), dma((2, C, PIECES)), dma((PIECES,)),
             dma((R + 1, PIECES)), dma((R, PIECES)),
         ],
@@ -294,16 +328,17 @@
             collective_id=0, has_side_effects=True, vmem_limit_bytes=56 * 1024 * 1024
         ),
         cost_estimate=pl.CostEstimate(
-            flops=2 * C * T * FC * FR, bytes_accessed=2 * FC * FR, transcendentals=0
+            flops=4 * C * T * FC * FR, bytes_accessed=4 * FC * FR, transcendentals=0
         ),
     )(context, d_out, out_weight)
 
 
 def on_device(R, C, context, d_out, out_weight):
-    context_rows, grad_rows, d_context = exchange(R, C, context, d_out, out_weight)
-    d_weight = lax.dot_general(
+    context_rows, grad_rows, d_context, half_weight = exchange(R, C, context, d_out, out_weight)
+    other_half = lax.dot_general(
         context_rows, grad_rows, (((0,), (0,)), ((), ())), preferred_element_type=jnp.float32
-    ).astype(jnp.bfloat16)
+    )
+    d_weight = (half_weight.astype(jnp.float32) + other_half).astype(jnp.bfloat16)
     return (d_context, d_weight)
 
 

time: 131 us -> 134 us (1.023)
  Pallas kernels: 102 us -> 109 us
  matrix products: 26.6 us -> 21.4 us
    pallas_call x1, Pallas kernels: 102 us -> 109 us  [exchange(): pl.pallas_call(functools.partial(kernel, R, C), out_shape=(jax.ShapeDtype...]
    dot_general x1, matrix products: 26.6 us -> 21.4 us  [on_device(): lax.dot_general(context_rows, grad_rows, (((0,), (0,)), ((), ())), prefer...]
where the time goes in v3:
time: 134 us; the launch traced here: 132 us
  Pallas kernels  109 us (81%)
  matrix products  21.4 us (16%)
    pallas_call x1, Pallas kernels, exchange(): pl.pallas_call(functools.partial(kernel, R, C), out_shape=(jax.ShapeDtype...  109 us
    dot_general x1, matrix products, on_device(): lax.dot_general(context_rows, grad_rows, (((0,), (0,)), ((), ())), prefer...  21.4 us

profile of v3, /device:TPU:10, one launch (start us, length us, event | category | flops | bytes accessed | tf_op | source)
XLA Modules:
  0.0 132.0 jit_solution(10554851522769157217)
XLA Ops:
  0.6 109.1 %shard_map.50 = (bf16[512,3072]{1,0:T(8,128)(2,1)}, bf16[512,3072]{1,0:T(8,128)(2,1)}, bf16[128,3072]{1,0:T(8,128)(2,1)}, bf16[3072,3072]{1,0:T(8,128)(2,1)}) custom-call(bf16[128,3072]{1,0:T(8,128)(2,1)} %ctx_in.1, bf16[128,3072]{1,0:T(8,128)(2,1)} %dout_in.1, bf16[3072,3072]{1,0:T(8,128)(2,1)} %w_in.1), custom_call_target="tpu_custom_call" | custom-call | flops 19327352832 | bytes 37748736 | tf_op jit(solution)/shard_map/pallas_call | solution.py:303
  109.7 0.0 copy-start
  109.7 21.4 %add_convert_fusion = bf16[3072,3072]{1,0:T(8,128)(2,1)} fusion(bf16[3072,3072]{1,0:T(8,128)(2,1)} %get-tuple-element.7, bf16[512,3072]{1,0:T(8,128)(2,1)} %get-tuple-element.8, bf16[512,3072]{1,0:T(8,128)(2,1)} %get-tuple-element.9), kind=kOutput, calls=%fused_computation | convolution fusion | flops 9691987968 | bytes 44040192 | tf_op jit(solution)/shard_map/dot_general | solution.py:338
  131.1 0.0 copy-done
  131.1 0.9 copy.6
Async XLA Ops:
  109.7 21.4 %copy-start = (bf16[128,3072]{1,0:T(8,128)(2,1)S(1)}, bf16[128,3072]{1,0:T(8,128)(2,1)}, u32[]{:S(2)}) copy-start(bf16[128,3072]{1,0:T(8,128)(2,1)} %get-tuple-element.12) | copy-start | bytes 2359300

commit v4 on v3

--- a/solution.py
+++ b/solution.py
@@ -27,8 +27,6 @@
     core = c - 2 * y
     mate = c + 1 - 2 * core
     halves = range(PIECES)
-    cuts = [(0, T // 8), (T // 8, T // 2 - T // 8), (T // 2, T // 2)]
-    late = range(1, 3)
 
     to_x, to_core = {"depth": 1 - x}, {"col": mate}
     to_right, to_left = {"row": z + 1}, {"row": z - 1}
@@ -70,7 +68,7 @@
         )
 
     def c_rows(r, p):
-        return pl.ds(r * T + cuts[p][0], cuts[p][1])
+        return rows(r, p)
 
     def c_copy(way, k, r, p, own=False):
         there = (cv, ctx_other)[k].at[c_rows(r, p)]
@@ -111,17 +109,16 @@
         pl.when(z < R - 1)(lambda: c_copy("right", k, z, p, own).start())
         pl.when(z > 0)(lambda: c_copy("left", k, z, p, own).start())
 
-    for p in range(3):
+    for p in halves:
         c_copy("x", 0, z, p, own=True).start()
         c_sends(0, p, own=True)
 
     def c_step(s):
         def arrived(r, way, more):
-            for k, p in ((0, 0), (0, 1), (0, 2), (1, 0)):
-                c_wait(k, r, p)
-                pl.when(more)(lambda: c_copy(way, k, r, p).start())
-                if p > 0:
-                    c_copy("x", 0, r, p).start()
+            for p in halves:
+                c_wait(0, r, p)
+                pl.when(more)(lambda: c_copy(way, 0, r, p).start())
+                c_copy("x", 0, r, p).start()
 
         pl.when(z - 1 - s >= 0)(lambda: arrived(z - 1 - s, "right", z < R - 1))
         pl.when(z + 1 + s <= R - 1)(lambda: arrived(z + 1 + s, "left", z > 0))
@@ -148,18 +145,49 @@
                 dv[tokens, :], wv[columns, :], (((1,), (1,)), ((), ())), preferred_element_type=jnp.float32
             )
 
+    def own_rows(slot, p):
+        return pl.ds(pl.multiple_of(slot * T + p * tp, tp), tp)
+
+    def r_copy(d, p, rightward):
+        if rightward:
+            return remote(sbuf.at[rows(d, p)], rbuf.at[rows(d, p)], r_send.at[d, p], r_recv.at[d, p], to_right)
+        slot = jnp.where(z - 1 == d, R, d)
+        return remote(sbuf.at[rows(d, p)], rbuf.at[rows(slot, p)], r_send.at[d, p], r_recv.at[slot, p], to_left)
+
+    def r_wait(slot, p):
+        there = rbuf.at[rows(slot, p)]
+        remote(there, there, r_send.at[0, p], r_recv.at[slot, p], to_x).wait_recv()
+
+    def r_hop(d, p, rightward, first):
+        here = own_rows(d, p)
+        if first:
+            sbuf[here, :] = part[here, :].astype(jnp.bfloat16)
+        else:
+            r_wait(d, p)
+            sbuf[here, :] = (part[here, :] + rbuf[here, :].astype(jnp.float32)).astype(jnp.bfloat16)
+        r_copy(d, p, rightward).start()
+
+    def r_begin(pair):
+        def both(d, rightward):
+            for p in halves:
+                r_hop(d, p, rightward, True)
+
+        for d in (2 * pair + 1, 2 * pair):
+            pl.when((z == 0) & (d > 0))(lambda: both(d, True))
+        for d in (2 * pair, 2 * pair + 1):
+            pl.when((z == R - 1) & (d < R - 1))(lambda: both(d, False))
+
     for p in halves:
         g_wait(0, mate, p)
     own_copies[0].wait()
     for copy in w_copies:
         copy.wait()
     multiply(y)
+    r_begin(y)
 
     for p in halves:
         g_wait(1, c, p)
         g_sends(1, c, p)
-    c_wait(1, z, 0)
-    c_sends(1, 0, own=False)
     c_step(0)
 
     def far_pair(s):
@@ -167,6 +195,7 @@
             for p in halves:
                 g_wait(0, 2 * pair + 1 - core, p)
             multiply(pair)
+            r_begin(pair)
 
         pl.when(y - 1 - s >= 0)(lambda: take(y - 1 - s))
         pl.when(y + 1 + s <= Y - 1)(lambda: take(y + 1 + s))
@@ -174,37 +203,6 @@
     for s in range(Y - 1):
         g_step(0, s)
         far_pair(s)
-
-    def r_copy(d, p, rightward):
-        if rightward:
-            return remote(sbuf.at[rows(d, p)], rbuf.at[rows(d, p)], r_send.at[d, p], r_recv.at[d, p], to_right)
-        slot = jnp.where(z - 1 == d, R, d)
-        return remote(sbuf.at[rows(d, p)], rbuf.at[rows(slot, p)], r_send.at[d, p], r_recv.at[slot, p], to_left)
-
-    def r_wait(slot, p):
-        there = rbuf.at[rows(slot, p)]
-        remote(there, there, r_send.at[0, p], r_recv.at[slot, p], to_x).wait_recv()
-
-    def r_hop(d, p, rightward, first):
-        if first:
-            sbuf[rows(d, p), :] = part[rows(d, p), :].astype(jnp.bfloat16)
-        else:
-            r_wait(d, p)
-            total = part[rows(d, p), :] + rbuf[rows(d, p), :].astype(jnp.float32)
-            sbuf[rows(d, p), :] = total.astype(jnp.bfloat16)
-        r_copy(d, p, rightward).start()
-
-    @pl.when(z == 0)
-    def _():
-        for d in range(R - 1, 0, -1):
-            for p in halves:
-                r_hop(d, p, True, True)
-
-    @pl.when(z == R - 1)
-    def _():
-        for d in range(R - 1):
-            for p in halves:
-                r_hop(d, p, False, True)
 
     for s in range(1, R - 1):
         c_step(s)
@@ -234,14 +232,14 @@
         stage_copy(i).start()
 
     for i in range(R - 1):
-        if i < stripes // 2:
-            stripe(i)
+        if i == 1:
+            stripe(0)
         for p in halves:
             pl.when((z > 0) & (z < R - 1 - i))(lambda: r_hop(R - 1 - i, p, True, False))
             pl.when((z < R - 1) & (z > i))(lambda: r_hop(i, p, False, False))
 
-    def own_rows(slot, p):
-        return pl.ds(pl.multiple_of(slot * T + p * tp, tp), tp)
+    for i in range(1, stripes):
+        stripe(i)
 
     for p in halves:
         out = pl.ds(p * tp, tp)
@@ -263,15 +261,13 @@
             both = rbuf[own_rows(z, p), :].astype(jnp.float32) + rbuf[own_rows(R, p), :].astype(jnp.float32)
             dctx[out, :] = (part[own_rows(z, p), :] + both).astype(jnp.bfloat16)
 
-    for i in range(min(R - 1, stripes // 2), stripes):
-        stripe(i)
     for i in range(max(stripes - 2, 0), stripes):
         stage_copy(i).wait()
 
     for p in halves:
         for b in range(Y):
             g_wait(1, 2 * b + 1 - core, p)
-    for p in late:
+    for p in halves:
         for r in range(R):
             c_wait(1, r, p)
     for p in halves:
@@ -284,14 +280,13 @@
                 pl.when((y > 0) & (b >= y))(lambda: g_copy("left", k, block, p).wait_send())
         for r in range(R):
             pl.when(z != r)(lambda: r_copy(r, p, True).wait_send())
-    c_copy("x", 0, z, 0).wait_send()
-    for p in late:
+    for p in halves:
         for r in range(R):
             c_copy("x", 0, r, p).wait_send()
-    for k, p in ((0, 0), (0, 1), (0, 2), (1, 0)):
+    for p in halves:
         for r in range(R):
-            pl.when((z < R - 1) & (r <= z))(lambda: c_copy("right", k, r, p).wait_send())
-            pl.when((z > 0) & (r >= z))(lambda: c_copy("left", k, r, p).wait_send())
+            pl.when((z < R - 1) & (r <= z))(lambda: c_copy("right", 0, r, p).wait_send())
+            pl.when((z > 0) & (r >= z))(lambda: c_copy("left", 0, r, p).wait_send())
 
 
 def exchange(R, C, context, d_out, out_weight):
@@ -320,7 +315,7 @@
             pltpu.VMEM((tn, R * T), bf16),
             pltpu.VMEM((2, tn, FR), bf16),
             dma((4,)), dma((2,)), dma((2,)),
-            dma((2, R, 3)), dma((2, R, 3)), dma((2, R, 3)), dma((R, 3)),
+            dma((2, R, PIECES)), dma((2, R, PIECES)), dma((2, R, PIECES)), dma((R, PIECES)),
             dma((2, C, PIECES)), dma((2, C, PIECES)), dma((2, C, PIECES)), dma((2, C, PIECES)), dma((PIECES,)),
             dma((R + 1, PIECES)), dma((R, PIECES)),
         ],
@@ -333,12 +328,38 @@
     )(context, d_out, out_weight)
 
 
+def add_half_kernel(context, grad, half, out):
+    turned = context[...].T
+    tn = 512 if grad.shape[1] % 512 == 0 else 256
+
+    @pl.loop(0, grad.shape[1] // tn)
+    def _(j):
+        columns = pl.ds(pl.multiple_of(j * tn, tn), tn)
+        product = jnp.dot(turned, grad[:, columns], preferred_element_type=jnp.float32)
+        out[:, columns] = (half[:, columns].astype(jnp.float32) + product).astype(jnp.bfloat16)
+
+
+def add_half(context, grad, half):
+    K, FC = context.shape
+    FR = grad.shape[1]
+    tm = 256
+    stripe = pl.BlockSpec((tm, FR), lambda i: (i, 0))
+    return pl.pallas_call(
+        add_half_kernel,
+        grid=(FC // tm,),
+        out_shape=jax.ShapeDtypeStruct((FC, FR), jnp.bfloat16),
+        in_specs=[pl.BlockSpec((K, tm), lambda i: (0, i)), pl.BlockSpec((K, FR), lambda i: (0, 0)), stripe],
+        out_specs=stripe,
+        compiler_params=pltpu.CompilerParams(vmem_limit_bytes=32 * 1024 * 1024),
+        cost_estimate=pl.CostEstimate(
+            flops=2 * K * FC * FR, bytes_accessed=4 * FC * FR, transcendentals=0
+        ),
+    )(context, grad, half)
+
+
 def on_device(R, C, context, d_out, out_weight):
     context_rows, grad_rows, d_context, half_weight = exchange(R, C, context, d_out, out_weight)
-    other_half = lax.dot_general(
-        context_rows, grad_rows, (((0,), (0,)), ((), ())), preferred_element_type=jnp.float32
-    )
-    d_weight = (half_weight.astype(jnp.float32) + other_half).astype(jnp.bfloat16)
+    d_weight = add_half(context_rows, grad_rows, half_weight)
     return (d_context, d_weight)
 
 

time: 134 us -> 134 us (level); the launches traced: 132 us -> 134 us
  matrix products: 21.4 us -> 0 us
  Pallas kernels: 109 us -> 129 us
  local copies, waits for them, and re-layouts: 0.88 us -> 4.65 us
    pallas_call x0 -> x1, Pallas kernels: none -> 27 us  [add_half(): pl.pallas_call(add_half_kernel, grid=(FC // tm,), out_shape=jax.ShapeDtyp...]
    dot_general x1 -> x0, matrix products: 21.4 us -> none  [on_device(): lax.dot_general(context_rows, grad_rows, (((0,), (0,)), ((), ())), prefer...]
    pallas_call x1, Pallas kernels: 109 us -> 102 us  [exchange(): pl.pallas_call(functools.partial(kernel, R, C), out_shape=(jax.ShapeDtype...]
    unnamed x3 -> x7, local copies, waits for them, and re-layouts: 0.88 us -> 4.65 us
where the time goes in v4:
time: 134 us
  Pallas kernels  129 us (96%)
  local copies, waits for them, and re-layouts  4.65 us (3%)
    pallas_call x1, Pallas kernels, exchange(): pl.pallas_call(functools.partial(kernel, R, C), out_shape=(jax.ShapeDtype...  102 us
    pallas_call x1, Pallas kernels, add_half(): pl.pallas_call(add_half_kernel, grid=(FC // tm,), out_shape=jax.ShapeDtyp...  27 us
    unnamed x7, local copies, waits for them, and re-layouts  4.65 us

profile of v4, /device:TPU:10, one launch (start us, length us, event | category | flops | bytes accessed | tf_op | source)
XLA Modules:
  0.0 134.1 jit_solution(2432516611570165224)
XLA Ops:
  0.6 101.8 %shard_map.50 = (bf16[512,3072]{1,0:T(8,128)(2,1)}, bf16[512,3072]{1,0:T(8,128)(2,1)}, bf16[128,3072]{1,0:T(8,128)(2,1)}, bf16[3072,3072]{1,0:T(8,128)(2,1)}) custom-call(bf16[128,3072]{1,0:T(8,128)(2,1)} %ctx_in.1, bf16[128,3072]{1,0:T(8,128)(2,1)} %dout_in.1, bf16[3072,3072]{1,0:T(8,128)(2,1)} %w_in.1), custom_call_target="tpu_custom_call" | custom-call | flops 19327352832 | bytes 37748736 | tf_op jit(solution)/shard_map/pallas_call | solution.py:298
  102.5 0.0 copy-start
  102.5 1.9 %copy-done = bf16[512,3072]{1,0:T(8,128)(2,1)S(1)} copy-done((bf16[512,3072]{1,0:T(8,128)(2,1)S(1)}, bf16[512,3072]{1,0:T(8,128)(2,1)}, u32[]{:S(2)}) %copy-start) | copy-done | bytes 3145752
  104.4 0.0 copy-start.1
  104.4 1.9 %copy-done.1 = bf16[512,3072]{1,0:T(8,128)(2,1)S(1)} copy-done((bf16[512,3072]{1,0:T(8,128)(2,1)S(1)}, bf16[512,3072]{1,0:T(8,128)(2,1)}, u32[]{:S(2)}) %copy-start.1) | copy-done | bytes 3145752
  106.3 0.0 copy-start.2
  106.3 27.0 %shard_map.51 = bf16[3072,3072]{1,0:T(8,128)(2,1)} custom-call(bf16[512,3072]{1,0:T(8,128)(2,1)S(1)} %copy-done, bf16[512,3072]{1,0:T(8,128)(2,1)S(1)} %copy-done.1, bf16[3072,3072]{1,0:T(8,128)(2,1)} %get-tuple-element.9.half), custom_call_target="tpu_custom_call" | custom-call | flops 9663676416 | bytes 37748736 | tf_op jit(solution)/shard_map/pallas_call | solution.py:347
  133.2 0.0 copy-done.2
  133.2 0.9 copy.6
Async XLA Ops:
  102.5 1.9 %copy-start = (bf16[512,3072]{1,0:T(8,128)(2,1)S(1)}, bf16[512,3072]{1,0:T(8,128)(2,1)}, u32[]{:S(2)}) copy-start(bf16[512,3072]{1,0:T(8,128)(2,1)} %get-tuple-element.7.context) | copy-start | bytes 9437188
  104.4 1.9 %copy-start.1 = (bf16[512,3072]{1,0:T(8,128)(2,1)S(1)}, bf16[512,3072]{1,0:T(8,128)(2,1)}, u32[]{:S(2)}) copy-start(bf16[512,3072]{1,0:T(8,128)(2,1)} %get-tuple-element.8.grad) | copy-start | bytes 9437188
  106.3 27.0 %copy-start.2 = (bf16[128,3072]{1,0:T(8,128)(2,1)S(1)}, bf16[128,3072]{1,0:T(8,128)(2,1)}, u32[]{:S(2)}) copy-start(bf16[128,3072]{1,0:T(8,128)(2,1)} %get-tuple-element.12) | copy-start | bytes 2359300
